TPU v7x, 128 devices: a whole 4x4x4 slice. The times are simulated.
128 devices in a mesh: row: 4 (over z_lo, core), col: 32 (over x, z_hi, y).
Axes of the slice: x: 4, y: 4, z: 4 (z_hi: 2, z_lo: 2; z = z_hi * 2 + z_lo), core: 2. Of those that a mesh axis runs over, the one named last changes fastest.
Arguments:
- visibilities: bfloat16 [32, 8, 1, 512, 512], P(None, None, None, 'col', 'row'), may hold values from -6 to 6
- coherencies: bfloat16 [32, 16, 8, 1, 512, 512], P(None, None, None, None, 'col', 'row'), may hold values from -1.1953125 to 1.1953125
- flags: int32 [32, 1, 512, 512], P(None, None, 'col', 'row'), may hold values 0 or 1
- freedom: int32 [512], replicated, may hold values from 2 to 12
- gains: float32 [32, 8, 16, 512], P(None, None, None, ('row', 'col')), may hold values from -4 to 4
Outputs:
- new_gains: float32 [32, 8, 16, 512], P(None, None, None, ('row', 'col'))
All inputs are finite; a program needn't handle non-finite values. No bound on the sum of `flags` on one device may be relied on, other than what follows from the above.
Results may differ from a plain program's by a relative error of at most 0.0003.
Values sent between devices are 32-bit elements; how exact they have to be, the bound alone decides.
A program may use at most 192 MiB of HBM per device.

v0:
```python
import jax
import jax.numpy as jnp
from jax import lax
from jax.sharding import PartitionSpec as P

damping = 1.0


def product(a, b):
    out = [None] * 8
    for i in range(2):
        for j in range(2):
            real = (
                a[2 * i] * b[j]
                - a[4 + 2 * i] * b[4 + j]
                + a[2 * i + 1] * b[2 + j]
                - a[5 + 2 * i] * b[6 + j]
            )
            imag = (
                a[2 * i] * b[4 + j]
                + a[4 + 2 * i] * b[j]
                + a[2 * i + 1] * b[6 + j]
                + a[5 + 2 * i] * b[2 + j]
            )
            out[2 * i + j] = real
            out[4 + 2 * i + j] = imag
    return out


def adjoint(a):
    out = [None] * 8
    for i in range(2):
        for j in range(2):
            out[2 * i + j] = a[2 * j + i]
            out[4 + 2 * i + j] = -a[4 + 2 * j + i]
    return out


def update(own, share):
    numer = [share[m] for m in range(8)]
    upper_a = share[8] + damping
    lower_d = share[9] + damping
    part_re = share[10]
    part_im = share[11]
    determ = upper_a * lower_d - part_re * part_re - part_im * part_im
    zeros = jnp.zeros_like(upper_a)
    inverse = [
        lower_d / determ,
        -part_re / determ,
        -part_re / determ,
        upper_a / determ,
        zeros,
        -part_im / determ,
        part_im / determ,
        zeros,
    ]
    step = product(numer, inverse)
    return own + jnp.stack(step)


def normal_terms(vis_c, coh_c, flag_c, gain_p, gain_q, nu_pair):
    coh_list = [coh_c[:, m].astype(jnp.float32) for m in range(8)]
    side_q = [gain_q[m][:, None, :, None] for m in range(8)]
    side_p = [gain_p[m][:, None, None, :] for m in range(8)]
    ylist = product(coh_list, adjoint(side_q))
    model = [jnp.sum(x, axis=0) for x in product(side_p, ylist)]
    resid = [vis_c[m].astype(jnp.float32) - model[m] for m in range(8)]
    energy = sum((x * x for x in resid))
    weight = flag_c.astype(jnp.float32) * (nu_pair + 8.0) / (nu_pair + energy)
    wres = [(weight * x)[None] for x in resid]
    numer = product(wres, adjoint(ylist))
    upper_a = weight * (ylist[0] ** 2 + ylist[4] ** 2 + ylist[1] ** 2 + ylist[5] ** 2)
    lower_d = weight * (ylist[2] ** 2 + ylist[6] ** 2 + ylist[3] ** 2 + ylist[7] ** 2)
    part_re = weight * (
        ylist[0] * ylist[2] + ylist[4] * ylist[6] + ylist[1] * ylist[3] + ylist[5] * ylist[7]
    )
    part_im = weight * (
        ylist[4] * ylist[2] - ylist[0] * ylist[6] + ylist[5] * ylist[3] - ylist[1] * ylist[7]
    )
    every = numer + [upper_a, lower_d, part_re, part_im]
    return jnp.stack([jnp.sum(x, axis=(1, 2)) for x in every])


def per_device(visibilities, coherencies, flags, freedom, gains):
    n_col = lax.axis_size("col")
    row_id = lax.axis_index("row")
    col_id = lax.axis_index("col")
    span_q = visibilities.shape[3]
    span_p = visibilities.shape[4]
    owned = span_p // n_col
    degree_p = lax.dynamic_slice_in_dim(freedom, row_id * span_p, span_p).astype(jnp.float32)
    degree_q = lax.dynamic_slice_in_dim(freedom, col_id * span_q, span_q).astype(jnp.float32)
    nu_pair = degree_q[:, None] + degree_p[None, :]
    every = lax.all_gather(gains, ("row", "col"), axis=3, tiled=True)
    gain_p = lax.dynamic_slice_in_dim(every, row_id * span_p, span_p, 3)
    gain_q = lax.dynamic_slice_in_dim(every, col_id * span_q, span_q, 3)

    def channel(pieces):
        vis_c, coh_c, flag_c, side_p, side_q = pieces
        return normal_terms(vis_c, coh_c, flag_c, side_p, side_q, nu_pair)

    partial_value = lax.map(channel, (visibilities, coherencies, flags, gain_p, gain_q))
    totals = lax.psum(partial_value, "col")
    share = lax.dynamic_slice_in_dim(totals, col_id * owned, owned, 3)

    def finish(pieces):
        own, part = pieces
        return update(own, part)

    return lax.map(finish, (gains, share))


def solution(mesh):
    return jax.shard_map(
        per_device,
        mesh=mesh,
        in_specs=(
            P(None, None, None, "col", "row"),
            P(None, None, None, None, "col", "row"),
            P(None, None, "col", "row"),
            P(),
            P(None, None, None, ("row", "col")),
        ),
        out_specs=P(None, None, None, ("row", "col")),
        check_vma=False,
    )
```

profile of v0, /device:TPU:0, one launch (start us, length us, event | category | flops | bytes accessed | tf_op | source)
XLA Modules:
  0.0 1054.4 jit_solution(5079816232408415774)
XLA Ops:
  6.5 1.7 copy.48
  9.8 350.2 %all-gather.2.cloned.1.call-done = f32[32,8,16,512]{0,2,1,3:T(8,128)} async-done(((f32[32,8,16,4]{0,2,1,3:T(8,128)}), f32[32,8,16,512]{0,2,1,3:T(8,128)}) %all-gather.2.cloned.1.call-update) | async-done | bytes 8388624 | tf_op jit(solution)/shard_map/all_gather | solution.py:94
  361.3 3.0 copy.51
  364.3 7.7 constant_dynamic-slice_fusion.22
  372.0 7.1 copy.49
  379.0 184.3 %while.22 = (s32[]{:T(128)}, f32[32,12,16,128]{3,2,1,0:T(8,128)}, s32[32,1,16,128]{3,2,1,0:T(8,128)}, bf16[32,8,1,16,128]{4,3,2,1,0:T(8,128)(2,1)}, f32[32,8,16,...) while((s32[]{:T(128)}, f32[32,12,16,128]{3,2,1,0:T(8,128)}, ...), condition=%wide.region_21.22_spmd.clone, body=%wide.region_0.21_spmd.clone.sunk | while | flops 7683081 | bytes 4797881 | solution.py:102
  565.5 359.4 %all-reduce.2.cloned.1.call-done = f32[32,12,16,128]{3,2,1,0:T(8,128)} async-done(((f32[32,12,16,128]{3,2,1,0:T(8,128)}), f32[32,12,16,128]{3,2,1,0:T(8,128)}) %all-reduce.2.cloned.1.call-update) | async-done | bytes 3145744 | tf_op jit(solution)/shard_map/psum | solution.py:103
  924.9 2.8 constant_dynamic-slice_fusion.20
  927.7 3.4 copy.53
  931.0 114.5 %while.21 = (s32[]{:T(128)}, f32[32,8,16,4]{2,1,3,0:T(8,128)}, f32[32,8,16,4]{2,1,3,0:T(8,128)}, f32[32,12,16,4]{2,3,1,0:T(4,128)}, s32[]{:T(128)}, /*index=5*/s...) while((s32[]{:T(128)}, f32[32,8,16,4]{2,1,3,0:T(8,128)}, ...), condition=%wide.region_24.25_spmd, body=%wide.region_23.24_spmd.sunk | while | flops 5069 | bytes 51853 | solution.py:110
  940.4 1.3 add_dynamic-update-slice_fusion.2
  944.0 1.3 add_dynamic-update-slice_fusion.2
  951.2 1.3 add_dynamic-update-slice_fusion.2
  969.1 1.3 add_dynamic-update-slice_fusion.2
  979.8 1.3 add_dynamic-update-slice_fusion.2
  987.0 1.3 add_dynamic-update-slice_fusion.2
  1001.3 1.3 add_dynamic-update-slice_fusion.2
  1012.0 1.3 add_dynamic-update-slice_fusion.2
  1022.8 1.3 add_dynamic-update-slice_fusion.2
  1026.3 1.3 add_dynamic-update-slice_fusion.2
  1029.9 1.3 add_dynamic-update-slice_fusion.2
  1037.1 1.3 add_dynamic-update-slice_fusion.2
  1040.6 1.3 add_dynamic-update-slice_fusion.2
  1045.5 2.0 copy.54
  (799 shorter events, 282.7 us)
Async XLA Ops:
  6.5 353.5 %all-gather.2.cloned.1.call-start = ((), (), s32[]{:S(2)}) async-start(), calls=%async_computation | async-start | bytes 33816576 | tf_op jit(solution)/shard_map/all_gather | solution.py:94
  8.2 916.7 %all-reduce.2.cloned.1.call-start = ((), (), s32[]{:S(2)}) async-start(), calls=%async_computation.1 | async-start | bytes 6291456 | tf_op jit(solution)/shard_map/psum | solution.py:103
  563.4 0.9 copy-start
Sparse Core Ops, SparseCore 0:
  9.0 350.8 all-gather.1
  563.5 361.3 all-reduce.1
where the time goes:
time: 1070 us; the launch traced here: 1050 us
  waiting for transfers between devices  710 us (66%)
  other arithmetic  239 us (22%)
  local copies, waits for them, and re-layouts  88.9 us (8%)
  between operations  13.4 us (1%)
    psum x1, waiting for transfers between devices, per_device(): totals = lax.psum(partial_value, 'col')  359 us
    all_gather x1, waiting for transfers between devices, per_device(): every = lax.all_gather(gains, ('row', 'col'), axis=3, tiled=True)  350 us
    add x96, other arithmetic, product(): a[2 * i] * b[4 + j] + a[4 + 2 * i] * b[j] + a[2 * i + 1] * b[6 + j]  70.6 us
    mul x64, other arithmetic, product(): a[2 * i] * b[j] - a[4 + 2 * i] * b[4 + j] + a[2 * i + 1] * b[2 + j]  56.4 us
    dynamic_update_slice x32, other arithmetic, per_device(): return lax.map(finish, (gains, share))  42.4 us
    squeeze x32, local copies, waits for them, and re-layouts, per_device(): lax.map(channel, (visibilities, coherencies, flags, gain_p, gain_q))  34.4 us
    mul x32, other arithmetic, product(): a[4 + 2 * i] * b[4 + j]  26 us
  transfers between devices with their start and end apart: 2, of which 2 were waited for; matrix products, arithmetic and copies ran while one was open for 0% of the time, Pallas kernels for 0%

commit v1 on v0

v1 whole, which is shorter than its diff:
```python
import jax
import jax.numpy as jnp
from jax import lax
from jax.experimental import pallas as pl
from jax.experimental.pallas import tpu as pltpu
from jax.sharding import PartitionSpec as P

F32 = jnp.float32
BF16 = jnp.bfloat16
MESH = pl.DeviceIdType.MESH
damping = 1.0


def product(a, b):
    out = [None] * 8
    for i in range(2):
        for j in range(2):
            real = (
                a[2 * i] * b[j]
                - a[4 + 2 * i] * b[4 + j]
                + a[2 * i + 1] * b[2 + j]
                - a[5 + 2 * i] * b[6 + j]
            )
            imag = (
                a[2 * i] * b[4 + j]
                + a[4 + 2 * i] * b[j]
                + a[2 * i + 1] * b[6 + j]
                + a[5 + 2 * i] * b[2 + j]
            )
            out[2 * i + j] = real
            out[4 + 2 * i + j] = imag
    return out


def prepare_gains(g, gq, gv, tab):
    a = g[:64]
    b = g[64:]
    gv[0] = a
    gv[1] = a + b
    gv[2] = b - a
    r = jnp.concatenate([gq] * 8, axis=0).T
    lane = lax.broadcasted_iota(jnp.int32, (16, 128), 1)
    sec = (lane // 16) % 4
    low = lane >= 64

    def pick(u0, u1, u2, u3):
        return jnp.where(sec == 0, u0, jnp.where(sec == 1, u1, jnp.where(sec == 2, u2, u3)))

    for j in range(2):
        r0, r1, i0, i1 = (r[m * 16 : m * 16 + 16] for m in (2 * j, 2 * j + 1, 4 + 2 * j, 5 + 2 * j))
        rows = [pick(r0, r1, i0, i1), pick(-i0, -i1, r0, r1), pick(r0 - i0, r1 - i1, i0 + r0, i1 + r1)]
        for v in range(3):
            hi = rows[v].astype(BF16).astype(F32)
            tab[j * 3 + v] = jnp.where(low, rows[v] - hi, hi)


def channel_sums(coh, vis, flag, nu, gv, tab, ys, wr, red, slab):
    lane = lax.broadcasted_iota(jnp.int32, (16, 128), 1)
    line = lax.broadcasted_iota(jnp.int32, (16, 128), 0)
    diag = (lane % 16) == line
    acc = [[jnp.zeros((16, 128), F32) for _ in range(3)] for _ in range(4)]
    for k in range(16):
        lhs = jnp.concatenate([jnp.where(diag, tab[g, k : k + 1, :], 0.0) for g in range(6)], axis=0).astype(BF16)
        half = jnp.concatenate(
            [
                jnp.concatenate([coh[k, 4 * ri + l], coh[k, 4 * ri + 2 + l]], axis=1)
                for ri in range(2)
                for l in range(2)
            ],
            axis=0,
        )
        out = jnp.dot(lhs, jnp.concatenate([half, half], axis=0), preferred_element_type=F32)
        y = {}
        for i in range(2):
            for j in range(2):
                for v in range(3):
                    t = out[(j * 3 + v) * 16 : (j * 3 + v) * 16 + 16, i * 128 : i * 128 + 128]
                    y[i, j, v] = t
                    ys[k, (i * 2 + j) * 3 + v] = t
        for i in range(2):
            for j in range(2):
                for l in range(2):
                    at = (2 * i + l) * 16 + k
                    ga, gs, gd = (gv[v, at : at + 1, :] for v in range(3))
                    part = acc[2 * i + j]
                    part[0] = part[0] + ga * y[l, j, 2]
                    part[1] = part[1] + gs * y[l, j, 1]
                    part[2] = part[2] + gd * y[l, j, 0]
    resid = []
    energy = None
    for m in range(4):
        re = vis[m].astype(F32) - (acc[m][0] - acc[m][1])
        im = vis[4 + m].astype(F32) - (acc[m][0] + acc[m][2])
        resid.append((re, im))
        t = re * re + im * im
        energy = t if energy is None else energy + t
    w = flag.astype(F32) * (nu + 8.0) / (nu + energy)
    for m in range(4):
        a = w * resid[m][0]
        b = w * resid[m][1]
        wr[m * 3] = a
        wr[m * 3 + 1] = a - b
        wr[m * 3 + 2] = a + b
    wr[12] = w
    for k in range(16):
        tot = [None] * 12
        cross = [[None] * 3 for _ in range(4)]
        for h in range(2):
            s = slice(8 * h, 8 * h + 8)
            y = [[[ys[k, (i * 2 + j) * 3 + v, s] for v in range(3)] for j in range(2)] for i in range(2)]
            for i in range(2):
                for j in range(2):
                    for l in range(2):
                        yr, yi, both = y[j][l]
                        at = (2 * i + l) * 3
                        terms = (wr[at, s] * both, wr[at + 1, s] * yi, wr[at + 2, s] * yr)
                        part = cross[2 * i + j]
                        for v in range(3):
                            part[v] = terms[v] if part[v] is None else part[v] + terms[v]
            (r00, i00, _), (r01, i01, _) = y[0]
            (r10, i10, _), (r11, i11, _) = y[1]
            every = (
                r00 * r00 + i00 * i00 + r01 * r01 + i01 * i01,
                r10 * r10 + i10 * i10 + r11 * r11 + i11 * i11,
                r00 * r10 + i00 * i10 + r01 * r11 + i01 * i11,
                i00 * r10 - r00 * i10 + i01 * r11 - r01 * i11,
            )
            for t in range(4):
                x = wr[12, s] * every[t]
                tot[8 + t] = x if h == 0 else tot[8 + t] + x
        for m in range(4):
            tot[m] = cross[m][0] - cross[m][1]
            tot[4 + m] = cross[m][2] - cross[m][0]
        for t in range(12):
            red[pl.ds((t * 16 + k) * 8, 8), :] = tot[t]
    for b in range(24):
        s = None
        for j in range(8):
            x = red[pl.ds(b * 64 + j, 8, stride=8), :]
            s = x if s is None else s + x
        slab[pl.ds(b * 8, 8), :] = s


def updated(g, total):
    share = [total[t * 16 : t * 16 + 16] for t in range(12)]
    upper_a = share[8] + damping
    lower_d = share[9] + damping
    part_re = share[10]
    part_im = share[11]
    determ = upper_a * lower_d - part_re * part_re - part_im * part_im
    zeros = jnp.zeros_like(upper_a)
    inverse = [
        lower_d / determ,
        -part_re / determ,
        -part_re / determ,
        upper_a / determ,
        zeros,
        -part_im / determ,
        part_im / determ,
        zeros,
    ]
    return g + jnp.concatenate(product(share[:8], inverse), axis=0)


def kernel(
    vis_hbm, coh_hbm, flag_hbm, free_ref, own_ref, fin,
    coh_v, vis_v, flag_v, ag, gqb, gv, tab, ys, wr, red, nu_v, gsv,
    slabs, r1, p1, r2, p2, r3, fsrc, f1,
    load_sem, s1_send, s1_recv, gq_send, gq_recv, s3_send, s3_recv,
    p1_send, p1_recv, p2_send, p2_recv, p3_send, p3_recv, f1_send, f1_recv, f2_send, f2_recv,
):
    row = lax.axis_index("row")
    col = lax.axis_index("col")
    x = col // 8
    z = (col // 4) % 2
    y = col % 4

    def col_of(xx, zz, yy):
        return xx * 8 + zz * 4 + yy

    def moved(t, da, dz, db):
        return col_of((x + (1 - t) * da + t * db) % 4, (z + dz) % 2, (y + t * da + (1 - t) * db) % 4)

    def axis_a(t):
        return x + t * (y - x)

    def axis_b(t):
        return y + t * (x - y)

    def step(n):
        t = n % 2
        s = (n // 2 + 1) % 4
        g = (n // 8 + 1) % 4
        alpha = (axis_a(t) + s) % 4
        beta = (axis_b(t) + g) % 4
        return t, g, s, alpha, beta

    def channel_of(t, alpha, beta):
        return (1 - t) * (alpha * 8 + beta) + t * (beta * 8 + 4 + alpha)

    def load(n):
        t, _, _, alpha, beta = step(n)
        return pltpu.make_async_copy(coh_hbm.at[channel_of(t, alpha, beta)], coh_v.at[n], load_sem.at[n])

    vis_copy = pltpu.make_async_copy(vis_hbm, vis_v, load_sem.at[32])
    flag_copy = pltpu.make_async_copy(flag_hbm, flag_v, load_sem.at[33])

    gq_row = x
    gq_cols = [col_of(z * 2 + y // 2, y % 2, m) for m in range(4)]
    gq_target = col_of(row, x // 2, (x % 2) * 2 + z)
    gq_here = [jnp.logical_and(gq_row == row, gq_cols[m] == col) for m in range(4)]
    gq_self = [jnp.logical_and(gq_target == col, row == r) for r in range(4)]
    is_self = (gq_target == col).astype(jnp.int32)

    peers = [moved(0, da, 0, 0) for da in (1, 2, 3)]
    peers += [moved(0, 0, dz, db) for dz in range(2) for db in range(4) if (dz, db) != (0, 0)]
    peers += [moved(0, da, 1, 0) for da in (1, 2, 3)]
    barrier = pltpu.get_barrier_semaphore()
    for peer in peers:
        pl.semaphore_signal(barrier, inc=1, device_id=(row, peer), device_id_type=MESH)
    for m in range(4):
        @pl.when(jnp.logical_not(gq_here[m]))
        def _():
            pl.semaphore_signal(barrier, inc=1, device_id=(gq_row, gq_cols[m]), device_id_type=MESH)

    lax.fori_loop(0, 2, lambda n, u: (load(n).start(), u)[1], 0)
    vis_copy.start()
    flag_copy.start()
    lax.fori_loop(2, 32, lambda n, u: (load(n).start(), u)[1], 0)

    for t in range(2):
        ag[t, :, :, axis_a(t), z, axis_b(t)] = own_ref[t]
    for m in range(4):
        @pl.when(gq_here[m])
        def _():
            for t in range(2):
                gqb[t, :, :, m] = own_ref[t]

    lane = lax.broadcasted_iota(jnp.int32, (16, 128), 1)
    line = lax.broadcasted_iota(jnp.int32, (16, 128), 0)
    free_q = jnp.broadcast_to(free_ref[pl.ds(x, 1), :].astype(F32), (16, 128))
    free_q = jnp.sum(jnp.where(lane == (z * 4 + y) * 16 + line, free_q, 0.0), axis=1, keepdims=True)
    nu_v[...] = free_q + free_ref[pl.ds(row, 1), :].astype(F32)

    pl.semaphore_wait(barrier, 17 - is_self)

    def s1(t, dz, db):
        at = t * 8 + dz * 4 + db
        return pltpu.make_async_remote_copy(
            src_ref=own_ref.at[t],
            dst_ref=ag.at[t, :, :, axis_a(t), z, axis_b(t)],
            send_sem=s1_send.at[at],
            recv_sem=s1_recv.at[at],
            device_id=(row, moved(t, 0, dz, db)),
            device_id_type=MESH,
        )

    def gq_copy(t, r):
        return pltpu.make_async_remote_copy(
            src_ref=own_ref.at[t],
            dst_ref=gqb.at[t, :, :, y],
            send_sem=gq_send.at[t * 4 + r],
            recv_sem=gq_recv.at[t * 4 + y],
            device_id=(r, gq_target),
            device_id_type=MESH,
        )

    def gq_arrival(t, m):
        return pltpu.make_async_remote_copy(
            src_ref=own_ref.at[t],
            dst_ref=gqb.at[t, :, :, m],
            send_sem=gq_send.at[t * 4],
            recv_sem=gq_recv.at[t * 4 + m],
            device_id=(gq_row, gq_cols[m]),
            device_id_type=MESH,
        )

    plane = [(dz, db) for dz in range(2) for db in range(4) if (dz, db) != (0, 0)]
    for dz, db in plane:
        for t in range(2):
            s1(t, dz, db).start()
    for r in range(4):
        @pl.when(jnp.logical_not(gq_self[r]))
        def _():
            for t in range(2):
                gq_copy(t, r).start()

    def s3(t, g, s):
        at = t * 16 + g * 4 + s
        block = ag.at[t, (axis_b(t) + g) % 4, :, axis_a(t)]
        return pltpu.make_async_remote_copy(
            src_ref=block,
            dst_ref=block,
            send_sem=s3_send.at[at],
            recv_sem=s3_recv.at[at],
            device_id=(row, moved(t, s, 0, 0)),
            device_id_type=MESH,
        )

    for t in range(2):
        for dz, db in plane:
            s1(t, dz, db).wait_recv()
    for g in (1, 2, 3, 0):
        for t in range(2):
            for s in (1, 2, 3):
                s3(t, g, s).start()
    for m in range(4):
        @pl.when(jnp.logical_not(gq_here[m]))
        def _():
            for t in range(2):
                gq_arrival(t, m).wait_recv()
    vis_copy.wait()
    flag_copy.wait()

    def send1(n):
        t, g, s, _, _ = step(n)
        at = t * 16 + g * 4 + s
        return pltpu.make_async_remote_copy(
            src_ref=slabs.at[n],
            dst_ref=r1.at[t, g, s - 1],
            send_sem=p1_send.at[at],
            recv_sem=p1_recv.at[at],
            device_id=(row, moved(t, s, 0, 0)),
            device_id_type=MESH,
        )

    def send2(t, g):
        at = t * 4 + g
        return pltpu.make_async_remote_copy(
            src_ref=p1.at[t, g],
            dst_ref=r2.at[t, g - 1],
            send_sem=p2_send.at[at],
            recv_sem=p2_recv.at[at],
            device_id=(row, moved(t, 0, 0, g)),
            device_id_type=MESH,
        )

    send3 = pltpu.make_async_remote_copy(
        src_ref=p2.at[1 - z],
        dst_ref=r3,
        send_sem=p3_send,
        recv_sem=p3_recv,
        device_id=(row, moved(0, 0, 1, 0)),
        device_id_type=MESH,
    )

    def sum1(t, gi):
        g = (gi + 1) % 4
        for i in range(3):
            send1(gi * 8 + 2 * i + t).wait_recv()
        p1[t, g] = slabs[gi * 8 + 6 + t] + r1[t, g, 0] + r1[t, g, 1] + r1[t, g, 2]

    def body(n, carry):
        t, g, s, alpha, beta = step(n)
        load(n).wait()

        @pl.when(s == 1)
        def _():
            for i in (1, 2, 3):
                s3(t, g, i).wait_recv()

        pieces = []
        for xx in range(4):
            for zz in range(2):
                for yy in range(4):
                    pieces.append(ag[t, beta, alpha, xx + t * (yy - xx), zz, yy + t * (xx - yy)])
        gains = jnp.concatenate(pieces, axis=0).T
        gq = jnp.concatenate([gqb[t, beta, alpha, m] for m in range(4)], axis=0)
        prepare_gains(gains, gq, gv, tab)

        @pl.when(n >= 30)
        def _():
            gsv[t] = gains

        c = channel_of(t, alpha, beta)
        channel_sums(
            coh_v.at[n], vis_v.at[c], flag_v[c], nu_v[...], gv, tab, ys, wr, red, slabs.at[n]
        )

        @pl.when(s != 0)
        def _():
            send1(n).start()

        @pl.when(jnp.logical_and(s == 2, n >= 8))
        def _():
            sum1(t, n // 8 - 1)
            send2(t, n // 8).start()

        return carry

    lax.fori_loop(0, 32, body, 0)

    for t in range(2):
        sum1(t, 3)
        for g in (1, 2, 3):
            send2(t, g).wait_recv()
        p2[t] = p1[t, 0] + r2[t, 0] + r2[t, 1] + r2[t, 2]
    send3.start()
    send3.wait_recv()
    fresh = updated(gsv[z], p2[z] + r3[...]).T
    for d in range(32):
        fsrc[d] = fresh[d * 4 : d * 4 + 4]

    def f1_copy(dx):
        return pltpu.make_async_remote_copy(
            src_ref=fsrc.at[pl.ds(((x + dx) % 4) * 8, 8)],
            dst_ref=f1.at[x],
            send_sem=f1_send.at[dx],
            recv_sem=f1_recv.at[dx],
            device_id=(row, moved(0, dx, 0, 0)),
            device_id_type=MESH,
        )

    def f2_copy(dz, dy):
        zz = (z + dz) % 2
        yy = (y + dy) % 4
        return pltpu.make_async_remote_copy(
            src_ref=f1.at[:, zz * 4 + yy],
            dst_ref=fin.at[:, z * 4 + y],
            send_sem=f2_send.at[dz * 4 + dy],
            recv_sem=f2_recv.at[dz * 4 + dy],
            device_id=(row, moved(0, 0, dz, dy)),
            device_id_type=MESH,
        )

    for dx in (1, 2, 3):
        f1_copy(dx).start()
    f1[x] = fsrc[pl.ds(x * 8, 8)]
    for dx in (1, 2, 3):
        f1_copy(dx).wait_recv()
    for dz, dy in plane:
        f2_copy(dz, dy).start()
    fin[:, z * 4 + y] = f1[:, z * 4 + y]
    for dz, dy in plane:
        f2_copy(dz, dy).wait_recv()

    for t in range(2):
        for dz, db in plane:
            s1(t, dz, db).wait_send()
    for r in range(4):
        @pl.when(jnp.logical_not(gq_self[r]))
        def _():
            for t in range(2):
                gq_copy(t, r).wait_send()
    for g in range(4):
        for t in range(2):
            for s in (1, 2, 3):
                s3(t, g, s).wait_send()

    def drain(n, carry):
        @pl.when((n // 2 + 1) % 4 != 0)
        def _():
            send1(n).wait_send()
        return carry

    lax.fori_loop(0, 32, drain, 0)
    for t in range(2):
        for g in (1, 2, 3):
            send2(t, g).wait_send()
    send3.wait_send()
    for dx in (1, 2, 3):
        f1_copy(dx).wait_send()
    for dz, dy in plane:
        f2_copy(dz, dy).wait_send()


def per_device(visibilities, coherencies, flags, freedom, gains):
    parts = jnp.transpose(gains.reshape(4, 2, 4, 128, 4), (1, 0, 2, 4, 3))
    own = jnp.stack([jnp.transpose(parts[0], (1, 0, 2, 3)), parts[1]])
    vmem = pl.BlockSpec(memory_space=pltpu.VMEM)
    hbm = pl.BlockSpec(memory_space=pl.ANY)
    dma = pltpu.SemaphoreType.DMA
    slab = (192, 128)
    fin = pl.pallas_call(
        kernel,
        out_shape=jax.ShapeDtypeStruct((4, 8, 4, 128), F32),
        in_specs=[hbm, hbm, hbm, vmem, vmem],
        out_specs=vmem,
        scratch_shapes=[
            pltpu.VMEM((32, 16, 8, 16, 128), BF16),
            pltpu.VMEM((32, 8, 16, 128), BF16),
            pltpu.VMEM((32, 16, 128), jnp.int32),
            pltpu.VMEM((2, 4, 4, 4, 2, 4, 4, 128), F32),
            pltpu.VMEM((2, 4, 4, 4, 4, 128), F32),
            pltpu.VMEM((3, 64, 128), F32),
            pltpu.VMEM((6, 16, 128), F32),
            pltpu.VMEM((16, 12, 16, 128), F32),
            pltpu.VMEM((13, 16, 128), F32),
            pltpu.VMEM((1536, 128), F32),
            pltpu.VMEM((16, 128), F32),
            pltpu.VMEM((2, 128, 128), F32),
            pltpu.VMEM((32,) + slab, F32),
            pltpu.VMEM((2, 4, 3) + slab, F32),
            pltpu.VMEM((2, 4) + slab, F32),
            pltpu.VMEM((2, 3) + slab, F32),
            pltpu.VMEM((2,) + slab, F32),
            pltpu.VMEM(slab, F32),
            pltpu.VMEM((32, 4, 128), F32),
            pltpu.VMEM((4, 8, 4, 128), F32),
            dma((34,)),
            dma((16,)), dma((16,)),
            dma((8,)), dma((8,)),
            dma((32,)), dma((32,)),
            dma((32,)), dma((32,)),
            dma((8,)), dma((8,)),
            dma, dma,
            dma((4,)), dma((4,)),
            dma((8,)), dma((8,)),
        ],
        compiler_params=pltpu.CompilerParams(
            collective_id=0, has_side_effects=True, vmem_limit_bytes=56 * 2**20
        ),
        cost_estimate=pl.CostEstimate(flops=10**9, bytes_accessed=2 * 10**7, transcendentals=0),
    )(
        visibilities.reshape(32, 8, 16, 128),
        coherencies.reshape(32, 16, 8, 16, 128),
        flags.reshape(32, 16, 128),
        freedom.reshape(4, 128),
        own,
    )
    return jnp.transpose(fin.reshape(32, 4, 8, 16), (0, 2, 3, 1))


def solution(mesh):
    return jax.shard_map(
        per_device,
        mesh=mesh,
        in_specs=(
            P(None, None, None, "col", "row"),
            P(None, None, None, None, "col", "row"),
            P(None, None, "col", "row"),
            P(),
            P(None, None, None, ("row", "col")),
        ),
        out_specs=P(None, None, None, ("row", "col")),
        check_vma=False,
    )
```

time: 1070 us -> 94.2 us (0.09); the launches traced: 1050 us -> 94 us
  waiting for transfers between devices: 710 us -> 0 us
  other arithmetic: 239 us -> 0.65 us
  Pallas kernels: 0 us -> 89.7 us
  local copies, waits for them, and re-layouts: 88.9 us -> 3.6 us
  between operations: 13.4 us -> 0.05 us
    psum x1 -> x0, waiting for transfers between devices: 359 us -> none  [per_device(): totals = lax.psum(partial_value, 'col')]
    all_gather x1 -> x0, waiting for transfers between devices: 350 us -> none  [per_device(): every = lax.all_gather(gains, ('row', 'col'), axis=3, tiled=True)]
    pallas_call x0 -> x1, Pallas kernels: none -> 89.7 us  [per_device(): pl.pallas_call(kernel, out_shape=jax.ShapeDtypeStruct((4, 8, 4, 128), F32...]
    mul x96 -> x0, other arithmetic: 82.3 us -> none  [the longest x64 56.4 us: product(): a[2 * i] * b[j] - a[4 + 2 * i] * b[4 + j] + a[2 * i + 1] * b[2 + j]]
    add x96 -> x0, other arithmetic: 70.6 us -> none  [product(): a[2 * i] * b[4 + j] + a[4 + 2 * i] * b[j] + a[2 * i + 1] * b[6 + j]]
    dynamic_update_slice x32 -> x0, other arithmetic: 42.4 us -> none  [per_device(): return lax.map(finish, (gains, share))]
    reduce_sum x64 -> x0, other arithmetic: 41.7 us -> none  [the longest x32 21.4 us: normal_terms(): return jnp.stack([jnp.sum(x, axis=(1, 2)) for x in every])]
    squeeze x32 -> x0, local copies, waits for them, and re-layouts: 34.4 us -> none  [per_device(): lax.map(channel, (visibilities, coherencies, flags, gain_p, gain_q))]
  transfers between devices with their start and end apart: 2 -> 0, of which waited for: 2 -> 0; matrix products, arithmetic and copies ran while one was open for 0% -> 0% of each run, Pallas kernels for 0% -> 0%
where the time goes in v1:
time: 94.2 us; the launch traced here: 94 us
  Pallas kernels  89.7 us (95%)
  local copies, waits for them, and re-layouts  3.6 us (4%)
    pallas_call x1, Pallas kernels, per_device(): pl.pallas_call(kernel, out_shape=jax.ShapeDtypeStruct((4, 8, 4, 128), F32...  89.7 us

profile of v1, /device:TPU:0, one launch (start us, length us, event | category | flops | bytes accessed | tf_op | source)
XLA Modules:
  0.0 94.0 jit_solution(17826361882903715101)
XLA Ops:
  0.0 1.4 %copy.8 = f32[32,8,16,4]{2,1,3,0:T(8,128)S(1)} copy(f32[32,8,16,4]{0,3,2,1:T(4,128)} %param.9) | data formatting | bytes 131072 | tf_op args[4]
  1.4 0.2 reshape.22
  1.7 0.6 pad_maximum_fusion.own_ref
  2.3 89.7 %shard_map.55 = f32[4,8,4,128]{3,2,1,0:T(4,128)} custom-call(bf16[32,8,16,128]{3,2,1,0:T(8,128)(2,1)} %bitcast.24, bf16[32,16,8,16,128]{4,3,2,1,0:T(8,128)(2,1)} %bitcast.22, s32[32,16,128]{2,1,0:T(8,128)} %bitcast.25, s32[4,128]{1,0:T(4,128)} %bitcast.27, f32[2,4,4,4,128]{4,3,2,1,0:T(4,128)} %pad_maximum_fusion.own_ref), custom_call_target="tpu_custom_call" | custom-call | flops 1000000000 | bytes 20000000 | tf_op jit(solution)/shard_map/pallas_call | solution.py:474
  92.0 0.8 copy.11
  92.9 0.2 reshape.23
  93.1 0.9 copy.12
  (2 shorter events, 0.0 us)

commit v2 on v1

--- a/solution.py
+++ b/solution.py
@@ -166,7 +166,7 @@
     vis_hbm, coh_hbm, flag_hbm, free_ref, own_ref, fin,
     coh_v, vis_v, flag_v, ag, gqb, gv, tab, ys, wr, red, nu_v, gsv,
     slabs, r1, p1, r2, p2, r3, fsrc, f1,
-    load_sem, s1_send, s1_recv, gq_send, gq_recv, s3_send, s3_recv,
+    gl, load_sem, s1_send, s1_recv, gq_send, gq_recv, s3_send, s3_recv,
     p1_send, p1_recv, p2_send, p2_recv, p3_send, p3_recv, f1_send, f1_recv, f2_send, f2_recv,
 ):
     row = lax.axis_index("row")
@@ -205,12 +205,10 @@
     vis_copy = pltpu.make_async_copy(vis_hbm, vis_v, load_sem.at[32])
     flag_copy = pltpu.make_async_copy(flag_hbm, flag_v, load_sem.at[33])
 
-    gq_row = x
-    gq_cols = [col_of(z * 2 + y // 2, y % 2, m) for m in range(4)]
-    gq_target = col_of(row, x // 2, (x % 2) * 2 + z)
-    gq_here = [jnp.logical_and(gq_row == row, gq_cols[m] == col) for m in range(4)]
-    gq_self = [jnp.logical_and(gq_target == col, row == r) for r in range(4)]
-    is_self = (gq_target == col).astype(jnp.int32)
+    gq_target = (y, col_of(row, x // 2, (x % 2) * 2 + z))
+    gq_source = (x, col_of(z * 2 + y // 2, y % 2, row))
+    gq_far = jnp.logical_or(gq_target[0] != row, gq_target[1] != col)
+    gq_from_far = jnp.logical_or(gq_source[0] != row, gq_source[1] != col)
 
     peers = [moved(0, da, 0, 0) for da in (1, 2, 3)]
     peers += [moved(0, 0, dz, db) for dz in range(2) for db in range(4) if (dz, db) != (0, 0)]
@@ -218,23 +216,32 @@
     barrier = pltpu.get_barrier_semaphore()
     for peer in peers:
         pl.semaphore_signal(barrier, inc=1, device_id=(row, peer), device_id_type=MESH)
-    for m in range(4):
-        @pl.when(jnp.logical_not(gq_here[m]))
-        def _():
-            pl.semaphore_signal(barrier, inc=1, device_id=(gq_row, gq_cols[m]), device_id_type=MESH)
+    for dr in (1, 2, 3):
+        pl.semaphore_signal(barrier, inc=1, device_id=((row + dr) % 4, col), device_id_type=MESH)
+
+    @pl.when(gq_from_far)
+    def _():
+        pl.semaphore_signal(barrier, inc=1, device_id=gq_source, device_id_type=MESH)
 
     lax.fori_loop(0, 2, lambda n, u: (load(n).start(), u)[1], 0)
     vis_copy.start()
     flag_copy.start()
     lax.fori_loop(2, 32, lambda n, u: (load(n).start(), u)[1], 0)
 
+    turned = jnp.concatenate([own_ref[:, p, :] for p in range(4)], axis=1).T
+    for p in range(4):
+        for cx in range(4):
+            for cy in range(4):
+                for t, beta, alpha in ((0, cy, cx), (1, cx, cy)):
+                    at = p * 32 + cx * 8 + t * 4 + cy
+                    gl[t, beta, alpha, p : p + 1] = turned[at : at + 1]
     for t in range(2):
-        ag[t, :, :, axis_a(t), z, axis_b(t)] = own_ref[t]
-    for m in range(4):
-        @pl.when(gq_here[m])
-        def _():
-            for t in range(2):
-                gqb[t, :, :, m] = own_ref[t]
+        ag[t, :, :, x, z, y] = gl[t]
+
+    @pl.when(jnp.logical_not(gq_from_far))
+    def _():
+        for t in range(2):
+            gqb[t, :, :, row] = gl[t]
 
     lane = lax.broadcasted_iota(jnp.int32, (16, 128), 1)
     line = lax.broadcasted_iota(jnp.int32, (16, 128), 0)
@@ -242,52 +249,70 @@
     free_q = jnp.sum(jnp.where(lane == (z * 4 + y) * 16 + line, free_q, 0.0), axis=1, keepdims=True)
     nu_v[...] = free_q + free_ref[pl.ds(row, 1), :].astype(F32)
 
-    pl.semaphore_wait(barrier, 17 - is_self)
-
-    def s1(t, dz, db):
-        at = t * 8 + dz * 4 + db
-        return pltpu.make_async_remote_copy(
-            src_ref=own_ref.at[t],
-            dst_ref=ag.at[t, :, :, axis_a(t), z, axis_b(t)],
+    pl.semaphore_wait(barrier, 16 + gq_far.astype(jnp.int32))
+
+    def s1(t, g, dz, db):
+        beta = (axis_b(t) + db + g) % 4
+        at = t * 32 + g * 8 + dz * 4 + db
+        return pltpu.make_async_remote_copy(
+            src_ref=gl.at[t, beta],
+            dst_ref=ag.at[t, beta, :, x, z, y],
             send_sem=s1_send.at[at],
             recv_sem=s1_recv.at[at],
             device_id=(row, moved(t, 0, dz, db)),
             device_id_type=MESH,
         )
 
-    def gq_copy(t, r):
-        return pltpu.make_async_remote_copy(
-            src_ref=own_ref.at[t],
-            dst_ref=gqb.at[t, :, :, y],
-            send_sem=gq_send.at[t * 4 + r],
-            recv_sem=gq_recv.at[t * 4 + y],
-            device_id=(r, gq_target),
-            device_id_type=MESH,
-        )
-
-    def gq_arrival(t, m):
-        return pltpu.make_async_remote_copy(
-            src_ref=own_ref.at[t],
-            dst_ref=gqb.at[t, :, :, m],
-            send_sem=gq_send.at[t * 4],
-            recv_sem=gq_recv.at[t * 4 + m],
-            device_id=(gq_row, gq_cols[m]),
-            device_id_type=MESH,
-        )
-
-    plane = [(dz, db) for dz in range(2) for db in range(4) if (dz, db) != (0, 0)]
-    for dz, db in plane:
-        for t in range(2):
-            s1(t, dz, db).start()
-    for r in range(4):
-        @pl.when(jnp.logical_not(gq_self[r]))
-        def _():
-            for t in range(2):
-                gq_copy(t, r).start()
+    def gq_copy(t, g):
+        second = (1 - t) * ((x % 2) * 2 + z) + t * row
+        beta = (second + g) % 4
+        return pltpu.make_async_remote_copy(
+            src_ref=gl.at[t, beta],
+            dst_ref=gqb.at[t, beta, :, y],
+            send_sem=gq_send.at[t * 16 + g * 4],
+            recv_sem=gq_recv.at[t * 16 + g * 4],
+            device_id=gq_target,
+            device_id_type=MESH,
+        )
+
+    def gq_arrival(t, g):
+        beta = (axis_b(t) + g) % 4
+        return pltpu.make_async_remote_copy(
+            src_ref=gl.at[t, beta],
+            dst_ref=gqb.at[t, beta, :, row],
+            send_sem=gq_send.at[t * 16 + g * 4],
+            recv_sem=gq_recv.at[t * 16 + g * 4],
+            device_id=gq_target,
+            device_id_type=MESH,
+        )
+
+    def gq_row_copy(t, g, dr):
+        beta = (axis_b(t) + g) % 4
+        block = gqb.at[t, beta, :, row]
+        return pltpu.make_async_remote_copy(
+            src_ref=block,
+            dst_ref=block,
+            send_sem=gq_send.at[t * 16 + g * 4 + dr],
+            recv_sem=gq_recv.at[t * 16 + g * 4 + dr],
+            device_id=((row + dr) % 4, col),
+            device_id_type=MESH,
+        )
+
+    def gq_row_arrival(t, g, dr):
+        beta = (axis_b(t) + g) % 4
+        return pltpu.make_async_remote_copy(
+            src_ref=gl.at[t, beta],
+            dst_ref=gqb.at[t, beta, :, (row + 4 - dr) % 4],
+            send_sem=gq_send.at[t * 16 + g * 4 + dr],
+            recv_sem=gq_recv.at[t * 16 + g * 4 + dr],
+            device_id=((row + dr) % 4, col),
+            device_id_type=MESH,
+        )
 
     def s3(t, g, s):
         at = t * 16 + g * 4 + s
-        block = ag.at[t, (axis_b(t) + g) % 4, :, axis_a(t)]
+        beta = (axis_b(t) + g) % 4
+        block = ag.at[0, beta, :, x] if t == 0 else ag.at[1, beta, :, :, :, y]
         return pltpu.make_async_remote_copy(
             src_ref=block,
             dst_ref=block,
@@ -297,18 +322,43 @@
             device_id_type=MESH,
         )
 
-    for t in range(2):
+    plane = [(dz, db) for dz in range(2) for db in range(4) if (dz, db) != (0, 0)]
+
+    def start_s1(g):
         for dz, db in plane:
-            s1(t, dz, db).wait_recv()
-    for g in (1, 2, 3, 0):
+            for t in range(2):
+                s1(t, g, dz, db).start()
+
+    def start_gq(g):
+        @pl.when(gq_far)
+        def _():
+            for t in range(2):
+                gq_copy(t, g).start()
+
+    def forward_gq(g):
+        @pl.when(gq_from_far)
+        def _():
+            for t in range(2):
+                gq_arrival(t, g).wait_recv()
+
         for t in range(2):
+            for dr in (1, 2, 3):
+                gq_row_copy(t, g, dr).start()
+
+    def start_s3(g):
+        for t in range(2):
+            for dz, db in plane:
+                s1(t, g, dz, db).wait_recv()
             for s in (1, 2, 3):
                 s3(t, g, s).start()
-    for m in range(4):
-        @pl.when(jnp.logical_not(gq_here[m]))
-        def _():
-            for t in range(2):
-                gq_arrival(t, m).wait_recv()
+
+    start_s1(1)
+    start_gq(1)
+    for g in (2, 3, 0):
+        start_s1(g)
+        start_gq(g)
+    start_s3(1)
+    forward_gq(1)
     vis_copy.wait()
     flag_copy.wait()
 
@@ -354,19 +404,20 @@
         t, g, s, alpha, beta = step(n)
         load(n).wait()
 
-        @pl.when(s == 1)
-        def _():
-            for i in (1, 2, 3):
-                s3(t, g, i).wait_recv()
-
-        pieces = []
-        for xx in range(4):
-            for zz in range(2):
-                for yy in range(4):
-                    pieces.append(ag[t, beta, alpha, xx + t * (yy - xx), zz, yy + t * (xx - yy)])
-        gains = jnp.concatenate(pieces, axis=0).T
-        gq = jnp.concatenate([gqb[t, beta, alpha, m] for m in range(4)], axis=0)
-        prepare_gains(gains, gq, gv, tab)
+        for tt in range(2):
+            @pl.when(jnp.logical_and(s == 1, t == tt))
+            def _():
+                for i in (1, 2, 3):
+                    s3(tt, g, i).wait_recv()
+                    gq_row_arrival(tt, g, i).wait_recv()
+
+        @pl.when(jnp.logical_and(n % 2 == 1, n < 6))
+        def _():
+            start_s3((n // 2 + 2) % 4)
+            forward_gq((n // 2 + 2) % 4)
+
+        gains = ag[t, beta, alpha].reshape(128, 128).T
+        prepare_gains(gains, gqb[t, beta, alpha].reshape(16, 128), gv, tab)
 
         @pl.when(n >= 30)
         def _():
@@ -434,18 +485,22 @@
     for dz, dy in plane:
         f2_copy(dz, dy).wait_recv()
 
-    for t in range(2):
-        for dz, db in plane:
-            s1(t, dz, db).wait_send()
-    for r in range(4):
-        @pl.when(jnp.logical_not(gq_self[r]))
-        def _():
-            for t in range(2):
-                gq_copy(t, r).wait_send()
-    for g in range(4):
+    def drain_gains(g, carry):
         for t in range(2):
+            for dz, db in plane:
+                s1(t, g, dz, db).wait_send()
             for s in (1, 2, 3):
                 s3(t, g, s).wait_send()
+            for dr in (1, 2, 3):
+                gq_row_copy(t, g, dr).wait_send()
+
+            @pl.when(gq_far)
+            def _():
+                gq_copy(t, g).wait_send()
+
+        return carry
+
+    lax.fori_loop(0, 4, drain_gains, 0)
 
     def drain(n, carry):
         @pl.when((n // 2 + 1) % 4 != 0)
@@ -465,8 +520,7 @@
 
 
 def per_device(visibilities, coherencies, flags, freedom, gains):
-    parts = jnp.transpose(gains.reshape(4, 2, 4, 128, 4), (1, 0, 2, 4, 3))
-    own = jnp.stack([jnp.transpose(parts[0], (1, 0, 2, 3)), parts[1]])
+    own = jnp.transpose(gains, (1, 2, 3, 0)).reshape(128, 4, 32)
     vmem = pl.BlockSpec(memory_space=pltpu.VMEM)
     hbm = pl.BlockSpec(memory_space=pl.ANY)
     dma = pltpu.SemaphoreType.DMA
@@ -497,9 +551,10 @@
             pltpu.VMEM(slab, F32),
             pltpu.VMEM((32, 4, 128), F32),
             pltpu.VMEM((4, 8, 4, 128), F32),
+            pltpu.VMEM((2, 4, 4, 4, 128), F32),
             dma((34,)),
-            dma((16,)), dma((16,)),
-            dma((8,)), dma((8,)),
+            dma((64,)), dma((64,)),
+            dma((32,)), dma((32,)),
             dma((32,)), dma((32,)),
             dma((32,)), dma((32,)),
             dma((8,)), dma((8,)),

time: 94.2 us -> 83.5 us (0.89)
  Pallas kernels: 89.7 us -> 81.4 us
  local copies, waits for them, and re-layouts: 3.6 us -> 1.96 us
    pallas_call x1, Pallas kernels: 89.7 us -> 81.4 us  [per_device(): pl.pallas_call(kernel, out_shape=jax.ShapeDtypeStruct((4, 8, 4, 128), F32...]
    unnamed x1 -> x0, local copies, waits for them, and re-layouts: 1.42 us -> none
where the time goes in v2:
time: 83.5 us; the launch traced here: 83.3 us
  Pallas kernels  81.4 us (97%)
  local copies, waits for them, and re-layouts  1.96 us (2%)
    pallas_call x1, Pallas kernels, per_device(): pl.pallas_call(kernel, out_shape=jax.ShapeDtypeStruct((4, 8, 4, 128), F32...  81.4 us

profile of v2, /device:TPU:0, one launch (start us, length us, event | category | flops | bytes accessed | tf_op | source)
XLA Modules:
  0.0 83.3 jit_solution(3220428980840137979)
XLA Ops:
  0.0 81.4 %shard_map.55 = f32[4,8,4,128]{3,2,1,0:T(4,128)} custom-call(bf16[32,8,16,128]{3,2,1,0:T(8,128)(2,1)} %bitcast.14, bf16[32,16,8,16,128]{4,3,2,1,0:T(8,128)(2,1)} %bitcast.12, s32[32,16,128]{2,1,0:T(8,128)} %bitcast.15, s32[4,128]{1,0:T(4,128)} %bitcast.17, f32[128,4,32]{2,1,0:T(4,128)} %bitcast.16), custom_call_target="tpu_custom_call" | custom-call | flops 1000000000 | bytes 20000000 | tf_op jit(solution)/shard_map/pallas_call | solution.py:528
  81.4 0.8 %copy.7 = f32[4,8,4,128]{3,1,0,2:T(8,128)S(1)} copy(f32[4,8,4,128]{3,2,1,0:T(4,128)} %shard_map.55) | data formatting | bytes 131072 | tf_op jit(solution)/shard_map/pallas_call | solution.py:528
  82.2 0.2 reshape.23
  82.4 0.9 %copy.8 = f32[32,8,16,4]{0,3,2,1:T(4,128)} copy(f32[32,8,16,4]{2,1,0,3:T(8,128)S(1)} %bitcast.13) | data formatting | bytes 131072 | tf_op jit(solution)/shard_map/transpose | solution.py:576

commit v3 on v2

--- a/solution.py
+++ b/solution.py
@@ -187,19 +187,35 @@
     def axis_b(t):
         return y + t * (x - y)
 
+    def relay_side(t, g):
+        return 1 + 2 * ((t + g) % 2)
+
+    lead = 4
+
+    def flag_of(cond):
+        return cond.astype(jnp.int32)
+
     def step(n):
-        t = n % 2
-        s = (n // 2 + 1) % 4
-        g = (n // 8 + 1) % 4
+        m = n - lead
+        first = flag_of(n < lead)
+        last = flag_of(n >= 32 - lead)
+        between = (1 - first) * (1 - last)
+        mine = last + between * (1 - m % 2)
+        j = first * n + last * (n - 16) + between * (m // 2 + (m % 2) * lead)
+        t = mine * z + (1 - mine) * (1 - z)
+        g = (j // 4 + 1) % 4
+        i = j % 4
+        d = relay_side(t, g)
+        s = 2 * flag_of(i == 0) + (4 - d) * flag_of(i == 1) + d * flag_of(i == 2)
         alpha = (axis_a(t) + s) % 4
         beta = (axis_b(t) + g) % 4
-        return t, g, s, alpha, beta
+        return t, j, g, s, alpha, beta
 
     def channel_of(t, alpha, beta):
         return (1 - t) * (alpha * 8 + beta) + t * (beta * 8 + 4 + alpha)
 
     def load(n):
-        t, _, _, alpha, beta = step(n)
+        t, _, _, _, alpha, beta = step(n)
         return pltpu.make_async_copy(coh_hbm.at[channel_of(t, alpha, beta)], coh_v.at[n], load_sem.at[n])
 
     vis_copy = pltpu.make_async_copy(vis_hbm, vis_v, load_sem.at[32])
@@ -324,53 +340,63 @@
 
     plane = [(dz, db) for dz in range(2) for db in range(4) if (dz, db) != (0, 0)]
 
-    def start_s1(g):
+    def by_type(t, act):
+        for tt in range(2):
+            @pl.when(t == tt)
+            def _():
+                act(tt)
+
+    def start_own(t, g):
         for dz, db in plane:
-            for t in range(2):
-                s1(t, g, dz, db).start()
-
-    def start_gq(g):
+            s1(t, g, dz, db).start()
+
         @pl.when(gq_far)
         def _():
-            for t in range(2):
-                gq_copy(t, g).start()
-
-    def forward_gq(g):
+            gq_copy(t, g).start()
+
+    def forward(t, g):
+        for dz, db in plane:
+            s1(t, g, dz, db).wait_recv()
+        for s in (1, 2, 3):
+            s3(t, g, s).start()
+
         @pl.when(gq_from_far)
         def _():
-            for t in range(2):
-                gq_arrival(t, g).wait_recv()
-
-        for t in range(2):
-            for dr in (1, 2, 3):
-                gq_row_copy(t, g, dr).start()
-
-    def start_s3(g):
-        for t in range(2):
-            for dz, db in plane:
-                s1(t, g, dz, db).wait_recv()
-            for s in (1, 2, 3):
-                s3(t, g, s).start()
-
-    start_s1(1)
-    start_gq(1)
-    for g in (2, 3, 0):
-        start_s1(g)
-        start_gq(g)
-    start_s3(1)
-    forward_gq(1)
+            gq_arrival(t, g).wait_recv()
+
+        for dr in (1, 2, 3):
+            gq_row_copy(t, g, dr).start()
+
+    kept = z
+    given = 1 - z
+    start_own(0, 1)
+    start_own(1, 1)
+    start_own(0, 2)
+    start_own(1, 2)
+    by_type(given, lambda t: forward(t, 1))
+    by_type(kept, lambda t: forward(t, 1))
     vis_copy.wait()
     flag_copy.wait()
 
-    def send1(n):
-        t, g, s, _, _ = step(n)
+    def send1(t, g, s, j):
         at = t * 16 + g * 4 + s
         return pltpu.make_async_remote_copy(
-            src_ref=slabs.at[n],
+            src_ref=slabs.at[t * 16 + j],
             dst_ref=r1.at[t, g, s - 1],
             send_sem=p1_send.at[at],
             recv_sem=p1_recv.at[at],
             device_id=(row, moved(t, s, 0, 0)),
+            device_id_type=MESH,
+        )
+
+    def relay(t, g, j):
+        at = t * 16 + g * 4
+        return pltpu.make_async_remote_copy(
+            src_ref=slabs.at[t * 16 + j],
+            dst_ref=r1.at[t, g, 1],
+            send_sem=p1_send.at[at],
+            recv_sem=p1_recv.at[at],
+            device_id=(row, moved(t, relay_side(t, g), 0, 0)),
             device_id_type=MESH,
         )
 
@@ -394,59 +420,96 @@
         device_id_type=MESH,
     )
 
-    def sum1(t, gi):
-        g = (gi + 1) % 4
-        for i in range(3):
-            send1(gi * 8 + 2 * i + t).wait_recv()
-        p1[t, g] = slabs[gi * 8 + 6 + t] + r1[t, g, 0] + r1[t, g, 1] + r1[t, g, 2]
-
-    def body(n, carry):
-        t, g, s, alpha, beta = step(n)
-        load(n).wait()
-
-        for tt in range(2):
-            @pl.when(jnp.logical_and(s == 1, t == tt))
-            def _():
-                for i in (1, 2, 3):
-                    s3(tt, g, i).wait_recv()
-                    gq_row_arrival(tt, g, i).wait_recv()
-
-        @pl.when(jnp.logical_and(n % 2 == 1, n < 6))
-        def _():
-            start_s3((n // 2 + 2) % 4)
-            forward_gq((n // 2 + 2) % 4)
-
-        gains = ag[t, beta, alpha].reshape(128, 128).T
-        prepare_gains(gains, gqb[t, beta, alpha].reshape(16, 128), gv, tab)
-
-        @pl.when(n >= 30)
-        def _():
-            gsv[t] = gains
-
-        c = channel_of(t, alpha, beta)
-        channel_sums(
-            coh_v.at[n], vis_v.at[c], flag_v[c], nu_v[...], gv, tab, ys, wr, red, slabs.at[n]
-        )
-
-        @pl.when(s != 0)
-        def _():
-            send1(n).start()
-
-        @pl.when(jnp.logical_and(s == 2, n >= 8))
-        def _():
-            sum1(t, n // 8 - 1)
-            send2(t, n // 8).start()
-
-        return carry
-
-    lax.fori_loop(0, 32, body, 0)
-
-    for t in range(2):
-        sum1(t, 3)
+    def sum1(t, g, j):
+        for i in (1, 3):
+            send1(t, g, i, 0).wait_recv()
+        p1[t, g] = slabs[t * 16 + j] + r1[t, g, 0] + r1[t, g, 2]
+
+        @pl.when(g % 3 == 0)
+        def _():
+            send1(t, g, 2, 0).wait_recv()
+            p1[t, g] = p1[t, g] + r1[t, g, 1]
+
+    def sum2(t):
+        sum1(t, 0, 15)
         for g in (1, 2, 3):
             send2(t, g).wait_recv()
         p2[t] = p1[t, 0] + r2[t, 0] + r2[t, 1] + r2[t, 2]
-    send3.start()
+
+    def body(n, carry):
+        t, j, g, s, alpha, beta = step(n)
+        i = j % 4
+        load(n).wait()
+
+        def at(*steps):
+            hit = n == steps[0]
+            for other in steps[1:]:
+                hit = jnp.logical_or(hit, n == other)
+            return pl.when(hit)
+
+        @at(0, 6, 14)
+        def _():
+            by_type(given, lambda tt: forward(tt, (2 + flag_of(n >= 6) + flag_of(n >= 14)) % 4))
+
+        @at(5, 13, 21)
+        def _():
+            by_type(kept, lambda tt: forward(tt, (2 + flag_of(n >= 13) + flag_of(n >= 21)) % 4))
+
+        @at(1, 8)
+        def _():
+            for tt in range(2):
+                start_own(tt, (3 + flag_of(n >= 8)) % 4)
+
+        for tt in range(2):
+            @pl.when(jnp.logical_and(i == 0, t == tt))
+            def _():
+                for k in (1, 2, 3):
+                    s3(tt, g, k).wait_recv()
+                    gq_row_arrival(tt, g, k).wait_recv()
+
+        gains = ag[t, beta, alpha].reshape(128, 128).T
+        prepare_gains(gains, gqb[t, beta, alpha].reshape(16, 128), gv, tab)
+
+        @pl.when(j == 15)
+        def _():
+            gsv[t] = gains
+
+        c = channel_of(t, alpha, beta)
+        channel_sums(
+            coh_v.at[n], vis_v.at[c], flag_v[c], nu_v[...], gv, tab, ys, wr, red, slabs.at[t * 16 + j]
+        )
+
+        direct = g % 3 == 0
+
+        @pl.when(jnp.logical_or(i == 1, jnp.logical_and(direct, i != 3)))
+        def _():
+            send1(t, g, s, j).start()
+
+        @pl.when(jnp.logical_and(jnp.logical_not(direct), i == 0))
+        def _():
+            relay(t, g, j).start()
+
+        @pl.when(jnp.logical_and(jnp.logical_not(direct), i == 3))
+        def _():
+            relay(t, g, j).wait_recv()
+            slabs[t * 16 + j - 1] = slabs[t * 16 + j - 1] + r1[t, g, 1]
+            send1(t, g, relay_side(t, g), j - 1).start()
+
+        @pl.when(jnp.logical_or(j == 6, jnp.logical_or(j == 10, j == 13)))
+        def _():
+            sum1(t, j // 4, (j // 4) * 4 - 1)
+            send2(t, j // 4).start()
+
+        @pl.when(n == 29)
+        def _():
+            sum2(given)
+            send3.start()
+
+        return carry
+
+    lax.fori_loop(0, 32, body, 0)
+
+    sum2(kept)
     send3.wait_recv()
     fresh = updated(gsv[z], p2[z] + r3[...]).T
     for d in range(32):
@@ -502,13 +565,22 @@
 
     lax.fori_loop(0, 4, drain_gains, 0)
 
-    def drain(n, carry):
-        @pl.when((n // 2 + 1) % 4 != 0)
-        def _():
-            send1(n).wait_send()
+    def drain(g, carry):
+        for t in range(2):
+            send1(t, g, 1, 0).wait_send()
+            send1(t, g, 3, 0).wait_send()
+
+            @pl.when(g % 3 == 0)
+            def _():
+                send1(t, g, 2, 0).wait_send()
+
+            @pl.when(g % 3 != 0)
+            def _():
+                relay(t, g, 0).wait_send()
+
         return carry
 
-    lax.fori_loop(0, 32, drain, 0)
+    lax.fori_loop(0, 4, drain, 0)
     for t in range(2):
         for g in (1, 2, 3):
             send2(t, g).wait_send()

time: 83.5 us -> 80.5 us (0.964)
  Pallas kernels: 81.4 us -> 78.4 us
    pallas_call x1, Pallas kernels: 81.4 us -> 78.4 us  [per_device(): pl.pallas_call(kernel, out_shape=jax.ShapeDtypeStruct((4, 8, 4, 128), F32...]
where the time goes in v3:
time: 80.5 us; the launch traced here: 80.3 us
  Pallas kernels  78.4 us (97%)
  local copies, waits for them, and re-layouts  1.96 us (2%)
    pallas_call x1, Pallas kernels, per_device(): pl.pallas_call(kernel, out_shape=jax.ShapeDtypeStruct((4, 8, 4, 128), F32...  78.4 us

profile of v3, /device:TPU:0, one launch (start us, length us, event | category | flops | bytes accessed | tf_op | source)
XLA Modules:
  0.0 80.3 jit_solution(3397318753386280954)
XLA Ops:
  0.0 78.4 %shard_map.55 = f32[4,8,4,128]{3,2,1,0:T(4,128)} custom-call(bf16[32,8,16,128]{3,2,1,0:T(8,128)(2,1)} %bitcast.14, bf16[32,16,8,16,128]{4,3,2,1,0:T(8,128)(2,1)} %bitcast.12, s32[32,16,128]{2,1,0:T(8,128)} %bitcast.15, s32[4,128]{1,0:T(4,128)} %bitcast.17, f32[128,4,32]{2,1,0:T(4,128)} %bitcast.16), custom_call_target="tpu_custom_call" | custom-call | flops 1000000000 | bytes 20000000 | tf_op jit(solution)/shard_map/pallas_call | solution.py:600
  78.4 0.8 %copy.7 = f32[4,8,4,128]{3,1,0,2:T(8,128)S(1)} copy(f32[4,8,4,128]{3,2,1,0:T(4,128)} %shard_map.55) | data formatting | bytes 131072 | tf_op jit(solution)/shard_map/pallas_call | solution.py:600
  79.2 0.2 reshape.23
  79.4 0.9 %copy.8 = f32[32,8,16,4]{0,3,2,1:T(4,128)} copy(f32[32,8,16,4]{2,1,0,3:T(8,128)S(1)} %bitcast.13) | data formatting | bytes 131072 | tf_op jit(solution)/shard_map/transpose | solution.py:648

commit v4 on v3

--- a/solution.py
+++ b/solution.py
@@ -389,17 +389,6 @@
             device_id_type=MESH,
         )
 
-    def relay(t, g, j):
-        at = t * 16 + g * 4
-        return pltpu.make_async_remote_copy(
-            src_ref=slabs.at[t * 16 + j],
-            dst_ref=r1.at[t, g, 1],
-            send_sem=p1_send.at[at],
-            recv_sem=p1_recv.at[at],
-            device_id=(row, moved(t, relay_side(t, g), 0, 0)),
-            device_id_type=MESH,
-        )
-
     def send2(t, g):
         at = t * 4 + g
         return pltpu.make_async_remote_copy(
@@ -421,14 +410,9 @@
     )
 
     def sum1(t, g, j):
-        for i in (1, 3):
+        for i in (1, 2, 3):
             send1(t, g, i, 0).wait_recv()
-        p1[t, g] = slabs[t * 16 + j] + r1[t, g, 0] + r1[t, g, 2]
-
-        @pl.when(g % 3 == 0)
-        def _():
-            send1(t, g, 2, 0).wait_recv()
-            p1[t, g] = p1[t, g] + r1[t, g, 1]
+        p1[t, g] = slabs[t * 16 + j] + r1[t, g, 0] + r1[t, g, 1] + r1[t, g, 2]
 
     def sum2(t):
         sum1(t, 0, 15)
@@ -479,23 +463,11 @@
             coh_v.at[n], vis_v.at[c], flag_v[c], nu_v[...], gv, tab, ys, wr, red, slabs.at[t * 16 + j]
         )
 
-        direct = g % 3 == 0
-
-        @pl.when(jnp.logical_or(i == 1, jnp.logical_and(direct, i != 3)))
+        @pl.when(i != 3)
         def _():
             send1(t, g, s, j).start()
 
-        @pl.when(jnp.logical_and(jnp.logical_not(direct), i == 0))
-        def _():
-            relay(t, g, j).start()
-
-        @pl.when(jnp.logical_and(jnp.logical_not(direct), i == 3))
-        def _():
-            relay(t, g, j).wait_recv()
-            slabs[t * 16 + j - 1] = slabs[t * 16 + j - 1] + r1[t, g, 1]
-            send1(t, g, relay_side(t, g), j - 1).start()
-
-        @pl.when(jnp.logical_or(j == 6, jnp.logical_or(j == 10, j == 13)))
+        @pl.when(jnp.logical_and(i == 1, j > 4))
         def _():
             sum1(t, j // 4, (j // 4) * 4 - 1)
             send2(t, j // 4).start()
@@ -508,45 +480,6 @@
         return carry
 
     lax.fori_loop(0, 32, body, 0)
-
-    sum2(kept)
-    send3.wait_recv()
-    fresh = updated(gsv[z], p2[z] + r3[...]).T
-    for d in range(32):
-        fsrc[d] = fresh[d * 4 : d * 4 + 4]
-
-    def f1_copy(dx):
-        return pltpu.make_async_remote_copy(
-            src_ref=fsrc.at[pl.ds(((x + dx) % 4) * 8, 8)],
-            dst_ref=f1.at[x],
-            send_sem=f1_send.at[dx],
-            recv_sem=f1_recv.at[dx],
-            device_id=(row, moved(0, dx, 0, 0)),
-            device_id_type=MESH,
-        )
-
-    def f2_copy(dz, dy):
-        zz = (z + dz) % 2
-        yy = (y + dy) % 4
-        return pltpu.make_async_remote_copy(
-            src_ref=f1.at[:, zz * 4 + yy],
-            dst_ref=fin.at[:, z * 4 + y],
-            send_sem=f2_send.at[dz * 4 + dy],
-            recv_sem=f2_recv.at[dz * 4 + dy],
-            device_id=(row, moved(0, 0, dz, dy)),
-            device_id_type=MESH,
-        )
-
-    for dx in (1, 2, 3):
-        f1_copy(dx).start()
-    f1[x] = fsrc[pl.ds(x * 8, 8)]
-    for dx in (1, 2, 3):
-        f1_copy(dx).wait_recv()
-    for dz, dy in plane:
-        f2_copy(dz, dy).start()
-    fin[:, z * 4 + y] = f1[:, z * 4 + y]
-    for dz, dy in plane:
-        f2_copy(dz, dy).wait_recv()
 
     def drain_gains(g, carry):
         for t in range(2):
@@ -565,18 +498,42 @@
 
     lax.fori_loop(0, 4, drain_gains, 0)
 
+    sum2(kept)
+    send3.wait_recv()
+    fresh = updated(gsv[z], p2[z] + r3[...]).T
+    for d in range(32):
+        fsrc[d] = fresh[d * 4 : d * 4 + 4]
+
+    def f1_copy(dx):
+        return pltpu.make_async_remote_copy(
+            src_ref=fsrc.at[pl.ds(((x + dx) % 4) * 8, 8)],
+            dst_ref=f1.at[x],
+            send_sem=f1_send.at[dx],
+            recv_sem=f1_recv.at[dx],
+            device_id=(row, moved(0, dx, 0, 0)),
+            device_id_type=MESH,
+        )
+
+    def f2_copy(dz, dy):
+        zz = (z + dz) % 2
+        yy = (y + dy) % 4
+        return pltpu.make_async_remote_copy(
+            src_ref=f1.at[:, zz * 4 + yy],
+            dst_ref=fin.at[:, z * 4 + y],
+            send_sem=f2_send.at[dz * 4 + dy],
+            recv_sem=f2_recv.at[dz * 4 + dy],
+            device_id=(row, moved(0, 0, dz, dy)),
+            device_id_type=MESH,
+        )
+
+    for dx in (1, 2, 3):
+        f1_copy(dx).start()
+    f1[x] = fsrc[pl.ds(x * 8, 8)]
+
     def drain(g, carry):
         for t in range(2):
-            send1(t, g, 1, 0).wait_send()
-            send1(t, g, 3, 0).wait_send()
-
-            @pl.when(g % 3 == 0)
-            def _():
-                send1(t, g, 2, 0).wait_send()
-
-            @pl.when(g % 3 != 0)
-            def _():
-                relay(t, g, 0).wait_send()
+            for i in (1, 2, 3):
+                send1(t, g, i, 0).wait_send()
 
         return carry
 
@@ -585,6 +542,14 @@
         for g in (1, 2, 3):
             send2(t, g).wait_send()
     send3.wait_send()
+    for dx in (1, 2, 3):
+        f1_copy(dx).wait_recv()
+    for dz, dy in plane:
+        f2_copy(dz, dy).start()
+    fin[:, z * 4 + y] = f1[:, z * 4 + y]
+    for dz, dy in plane:
+        f2_copy(dz, dy).wait_recv()
+
     for dx in (1, 2, 3):
         f1_copy(dx).wait_send()
     for dz, dy in plane:

time: 80.5 us -> 78.8 us (0.979)
  Pallas kernels: 78.4 us -> 76.6 us
    pallas_call x1, Pallas kernels: 78.4 us -> 76.6 us  [per_device(): pl.pallas_call(kernel, out_shape=jax.ShapeDtypeStruct((4, 8, 4, 128), F32...]
where the time goes in v4:
time: 78.8 us; the launch traced here: 78.6 us
  Pallas kernels  76.6 us (97%)
  local copies, waits for them, and re-layouts  1.96 us (2%)
    pallas_call x1, Pallas kernels, per_device(): pl.pallas_call(kernel, out_shape=jax.ShapeDtypeStruct((4, 8, 4, 128), F32...  76.6 us

profile of v4, /device:TPU:0, one launch (start us, length us, event | category | flops | bytes accessed | tf_op | source)
XLA Modules:
  0.0 78.6 jit_solution(17897773184545934410)
XLA Ops:
  0.0 76.6 %shard_map.55 = f32[4,8,4,128]{3,2,1,0:T(4,128)} custom-call(bf16[32,8,16,128]{3,2,1,0:T(8,128)(2,1)} %bitcast.14, bf16[32,16,8,16,128]{4,3,2,1,0:T(8,128)(2,1)} %bitcast.12, s32[32,16,128]{2,1,0:T(8,128)} %bitcast.15, s32[4,128]{1,0:T(4,128)} %bitcast.17, f32[128,4,32]{2,1,0:T(4,128)} %bitcast.16), custom_call_target="tpu_custom_call" | custom-call | flops 1000000000 | bytes 20000000 | tf_op jit(solution)/shard_map/pallas_call | solution.py:565
  76.6 0.8 %copy.7 = f32[4,8,4,128]{3,1,0,2:T(8,128)S(1)} copy(f32[4,8,4,128]{3,2,1,0:T(4,128)} %shard_map.55) | data formatting | bytes 131072 | tf_op jit(solution)/shard_map/pallas_call | solution.py:565
  77.5 0.2 reshape.23
  77.7 0.9 %copy.8 = f32[32,8,16,4]{0,3,2,1:T(4,128)} copy(f32[32,8,16,4]{2,1,0,3:T(8,128)S(1)} %bitcast.13) | data formatting | bytes 131072 | tf_op jit(solution)/shard_map/transpose | solution.py:613

commit v5 on v4

--- a/solution.py
+++ b/solution.py
@@ -371,9 +371,9 @@
     given = 1 - z
     start_own(0, 1)
     start_own(1, 1)
+    by_type(given, lambda t: forward(t, 1))
     start_own(0, 2)
     start_own(1, 2)
-    by_type(given, lambda t: forward(t, 1))
     by_type(kept, lambda t: forward(t, 1))
     vis_copy.wait()
     flag_copy.wait()

time: 78.8 us -> 82.5 us (1.047)
  Pallas kernels: 76.6 us -> 80.4 us
    pallas_call x1, Pallas kernels: 76.6 us -> 80.4 us  [per_device(): pl.pallas_call(kernel, out_shape=jax.ShapeDtypeStruct((4, 8, 4, 128), F32...]
where the time goes in v5:
time: 82.5 us; the launch traced here: 82.3 us
  Pallas kernels  80.4 us (97%)
  local copies, waits for them, and re-layouts  1.96 us (2%)
    pallas_call x1, Pallas kernels, per_device(): pl.pallas_call(kernel, out_shape=jax.ShapeDtypeStruct((4, 8, 4, 128), F32...  80.4 us

profile of v5, /device:TPU:0, one launch (start us, length us, event | category | flops | bytes accessed | tf_op | source)
XLA Modules:
  0.0 82.3 jit_solution(7410944249447268546)
XLA Ops:
  0.0 80.4 %shard_map.55 = f32[4,8,4,128]{3,2,1,0:T(4,128)} custom-call(bf16[32,8,16,128]{3,2,1,0:T(8,128)(2,1)} %bitcast.14, bf16[32,16,8,16,128]{4,3,2,1,0:T(8,128)(2,1)} %bitcast.12, s32[32,16,128]{2,1,0:T(8,128)} %bitcast.15, s32[4,128]{1,0:T(4,128)} %bitcast.17, f32[128,4,32]{2,1,0:T(4,128)} %bitcast.16), custom_call_target="tpu_custom_call" | custom-call | flops 1000000000 | bytes 20000000 | tf_op jit(solution)/shard_map/pallas_call | solution.py:565
  80.4 0.8 %copy.7 = f32[4,8,4,128]{3,1,0,2:T(8,128)S(1)} copy(f32[4,8,4,128]{3,2,1,0:T(4,128)} %shard_map.55) | data formatting | bytes 131072 | tf_op jit(solution)/shard_map/pallas_call | solution.py:565
  81.2 0.2 reshape.23
  81.4 0.9 %copy.8 = f32[32,8,16,4]{0,3,2,1:T(4,128)} copy(f32[32,8,16,4]{2,1,0,3:T(8,128)S(1)} %bitcast.13) | data formatting | bytes 131072 | tf_op jit(solution)/shard_map/transpose | solution.py:613
